TPU v7x, 1024 devices: a whole 4x4x32 slice. The times are simulated.
1024 devices in a mesh: row: 16 (over z_hi, y), col: 64 (over z_lo, x, core).
Axes of the slice: x: 4, y: 4, z: 32 (z_hi: 4, z_lo: 8; z = z_hi * 8 + z_lo), core: 2. Of those that a mesh axis runs over, the one named last changes fastest.
Arguments:
- hamiltonian: bfloat16 [24576, 24576], P('row', 'col'), as said below
- pattern: int32 [192, 192], P('row', 'col'), may hold values from 0 to 1, as said below
- vectors: bfloat16 [24576, 256], P('col'), may hold values from -6 to 6
Outputs:
- filtered: bfloat16 [24576, 256], P(('row', 'col'))
Inputs may be any that keep to these rules, and one draw needn't show every extreme that they name: hamiltonian is exactly symmetric. pattern is symmetric, with ones on the diagonal and next to it.
All inputs are finite; a program needn't handle non-finite values.
Results may differ from a plain program's by a relative error of at most 0.018.
Values may be sent and summed in bfloat16 or wider, within the bound.
A program may use at most 32 MiB of HBM per device.

v0:
```python
import jax
import jax.numpy as jnp
from jax import lax
from jax.sharding import PartitionSpec as P

ORB = 128


def apply_mask(hamiltonian, pattern):
    rows_here, cols_here = hamiltonian.shape
    blocks = hamiltonian.reshape(rows_here // ORB, ORB, cols_here // ORB, ORB)
    return (blocks * pattern.astype(jnp.bfloat16)[:, None, :, None]).reshape(rows_here, cols_here)


def body(hamiltonian, pattern, vectors):
    masked = apply_mask(hamiltonian, pattern)
    rows_here, cols_here = masked.shape
    col_count = lax.axis_size("col")
    piece_len = rows_here // col_count
    row_idx = lax.axis_index("row")

    def col_scatter(partial_value):
        return lax.psum_scatter(partial_value, "col", scatter_dimension=0, tiled=True)

    partial_value = jnp.dot(masked, vectors, preferred_element_type=jnp.float32)
    first_piece = col_scatter(partial_value).astype(jnp.bfloat16)
    product = lax.dot_general(
        masked,
        lax.all_gather(first_piece, "col", axis=0, tiled=True),
        (((0,), (0,)), ((), ())),
        preferred_element_type=jnp.float32,
    )
    own_share = lax.psum_scatter(
        product.astype(jnp.bfloat16), "row", scatter_dimension=0, tiled=True
    ).astype(jnp.float32)
    own_rows = lax.dynamic_slice_in_dim(vectors, row_idx * piece_len, piece_len, 0)
    second_piece = (2.0 * own_share - own_rows.astype(jnp.float32)).astype(jnp.bfloat16)
    partial_value = jnp.dot(
        masked,
        lax.all_gather(second_piece, "row", axis=0, tiled=True),
        preferred_element_type=jnp.float32,
    )
    third = col_scatter(partial_value)
    return (2.0 * third - first_piece.astype(jnp.float32)).astype(jnp.bfloat16)


def solution(mesh):
    in_specs = (P("row", "col"), P("row", "col"), P("col", None))
    out_specs = P(("row", "col"), None)
    return jax.shard_map(body, mesh=mesh, in_specs=in_specs, out_specs=out_specs, check_vma=False)
```

profile of v0, /device:TPU:24, one launch (start us, length us, event | category | flops | bytes accessed | tf_op | source)
XLA Modules:
  0.0 1272.5 jit_solution(14134029986667919208)
XLA Ops:
  6.5 0.0 reduce-scatter.4.cloned.1.call-start
  6.5 0.7 convert_element_type.24
  7.2 1.6 copy.5
  8.8 0.3 mul.20
  9.1 0.0 copy-start
  9.1 0.3 bitcast_multiply_fusion
  9.3 0.7 copy-done
  10.0 1.8 fusion
  11.8 0.0 reduce-scatter.4.cloned.1.call-update
  11.8 0.0 reduce-scatter.6.cloned.1.call-start
  11.9 455.7 %reduce-scatter.4.cloned.1.call-done = f32[24,256]{1,0:T(8,128)} async-done(((f32[1536,256]{1,0:T(8,128)}), f32[24,256]{1,0:T(8,128)}) %reduce-scatter.4.cloned.1.call-update) | async-done | bytes 24592 | tf_op jit(solution)/shard_map/reduce_scatter | solution.py:23
  467.6 0.7 convert_element_type.25
  468.3 114.2 %all_gather.6 = bf16[1536,256]{1,0:T(8,128)(2,1)S(1)} all-gather(bf16[24,256]{1,0:T(8,128)(2,1)S(1)} %convert_element_type.25), channel_id=1, replica_groups=mesh['row'=16,'col'=64] {'col'}, dimensions={0}, use_global_device_ids=true | all-gather | bytes 798720 | tf_op jit(solution)/shard_map/all_gather | solution.py:29
  582.5 1.1 convolution_convert_fusion
  583.7 0.0 reduce-scatter.6.cloned.1.call-update
  583.7 0.0 reduce-scatter.8.cloned.1.call-start
  583.7 162.4 %reduce-scatter.6.cloned.1.call-done = bf16[24,256]{1,0:T(8,128)(2,1)} async-done(((bf16[384,256]{1,0:T(8,128)(2,1)}), bf16[24,256]{1,0:T(8,128)(2,1)}) %reduce-scatter.6.cloned.1.call-update) | async-done | bytes 12304 | tf_op jit(solution)/shard_map/reduce_scatter | solution.py:33
  746.2 0.7 subtract_convert_fusion.1
  746.9 66.3 %all_gather.7 = bf16[384,256]{1,0:T(8,128)(2,1)S(1)} all-gather(bf16[24,256]{1,0:T(8,128)(2,1)S(1)} %subtract_convert_fusion.1), channel_id=1, replica_groups=mesh['row'=16,'col'=64] {'row'}, dimensions={0}, use_global_device_ids=true | all-gather | bytes 208896 | tf_op jit(solution)/shard_map/all_gather | solution.py:40
  813.1 1.8 fusion.1
  814.9 0.0 reduce-scatter.8.cloned.1.call-update
  814.9 449.6 %reduce-scatter.8.cloned.1.call-done = f32[24,256]{1,0:T(8,128)} async-done(((f32[1536,256]{1,0:T(8,128)}), f32[24,256]{1,0:T(8,128)}) %reduce-scatter.8.cloned.1.call-update) | async-done | bytes 24592 | tf_op jit(solution)/shard_map/reduce_scatter | solution.py:23
  1264.6 0.0 copy-done.1
  1264.6 1.3 subtract_convert_fusion
  (1 shorter events, 0.0 us)
Async XLA Ops:
  6.5 461.1 %reduce-scatter.4.cloned.1.call-start = ((), (), s32[]{:S(2)}) async-start(), calls=%async_computation.3 | async-start | bytes 1597440 | tf_op jit(solution)/shard_map/reduce_scatter | solution.py:23
  9.1 0.9 copy-start
  11.8 734.3 %reduce-scatter.6.cloned.1.call-start = ((), (), s32[]{:S(2)}) async-start(), calls=%async_computation.4 | async-start | bytes 208896 | tf_op jit(solution)/shard_map/reduce_scatter | solution.py:33
  583.7 680.9 %reduce-scatter.8.cloned.1.call-start = ((), (), s32[]{:S(2)}) async-start(), calls=%async_computation.5 | async-start | bytes 1597440 | tf_op jit(solution)/shard_map/reduce_scatter | solution.py:23
  814.9 449.7 %copy-start.1 = (f32[24,256]{1,0:T(8,128)S(1)}, f32[24,256]{1,0:T(8,128)}, u32[]{:S(2)}) copy-start(f32[24,256]{1,0:T(8,128)} %reduce-scatter.4.cloned.1.call-done) | copy-start | bytes 73732
Sparse Core Ops, SparseCore 0:
  11.9 455.6 reduce-scatter.3
  583.8 162.3 reduce-scatter.5
  815.1 449.4 reduce-scatter.7
where the time goes:
time: 1270 us
  waiting for transfers between devices  1070 us (84%)
  blocking collectives  180 us (14%)
  between operations  13.1 us (1%)
    reduce_scatter x2, waiting for transfers between devices, col_scatter(): lax.psum_scatter(partial_value, 'col', scatter_dimension=0, tiled=True)  905 us
    reduce_scatter x1, waiting for transfers between devices, body(): lax.psum_scatter(product.astype(jnp.bfloat16), 'row', scatter_dimension=0...  162 us
    all_gather x1, blocking collectives, body(): lax.all_gather(first_piece, 'col', axis=0, tiled=True)  114 us
    all_gather x1, blocking collectives, body(): lax.all_gather(second_piece, 'row', axis=0, tiled=True)  66.3 us
  transfers between devices with their start and end apart: 3, of which 3 were waited for; matrix products, arithmetic and copies ran while one was open for 0% of the time, Pallas kernels for 0%

commit v1 on v0

v1 whole, which is shorter than its diff:
```python
import functools

import jax
import jax.numpy as jnp
from jax import lax
from jax.experimental import pallas as pl
from jax.experimental.pallas import tpu as pltpu
from jax.sharding import PartitionSpec as P

MESH = pl.DeviceIdType.MESH
F32, BF16 = jnp.float32, jnp.bfloat16
ORB = 128
NX, NZ, NY, NW = 4, 8, 4, 4
PIECE = 24
STACK = NZ * PIECE
HALF = NX * STACK
ROWS = 2 * HALF
COLS = 384
WIDTH = 256
CHUNKS = 2
W = WIDTH // CHUNKS
MIDDLE = 2 * PIECE
QUARTER = COLS // NY
PAIR = QUARTER // 2


def kernel(
    h_hbm, pat_ref, v_ref, out_ref,
    raw, wide, ham, ham_t, own, acc, accy, firstw,
    send_c, recv_c, send_x, recv_x, send_z, recv_z, first,
    send_y, recv_y, send_w, recv_w, second, send_f, recv_f,
    send_sem, recv_sem, load_sem,
):
    col, row = lax.axis_index("col"), lax.axis_index("row")
    core, x, z = lax.rem(col, 2), lax.rem(lax.div(col, 2), NX), lax.div(col, 2 * NX)
    y, w = lax.rem(row, NY), lax.div(row, NY)

    def device(core=core, x=x, z=z, y=y, w=w):
        return {"row": w * NY + y, "col": (z * NX + x) * 2 + core}

    def plus(at, d, n):
        return lax.rem(at + d, n)

    def minus(at, d, n):
        return lax.rem(at + n - d, n)

    def rows_at(start, size, unit):
        return pl.ds(pl.multiple_of(start, unit), size)

    other = device(core=1 - core)
    x_peer = {d: device(x=plus(x, d, NX)) for d in range(1, NX)}
    z_peer = {d: device(z=plus(z, d, NZ)) for d in range(1, NZ)}
    y_peer = {d: device(y=plus(y, d, NY)) for d in range(1, NY)}
    w_peer = [device(w=w + 1 - 2 * lax.rem(w, 2)), device(w=NW - 1 - w)]
    everyone = [other, *x_peer.values(), *z_peer.values(), *y_peer.values(), *w_peer]

    barrier = pltpu.get_barrier_semaphore()
    for peer in everyone:
        pl.semaphore_signal(barrier, inc=1, device_id=peer, device_id_type=MESH)

    used = []

    def copy(src, dst, slot, peer):
        return pltpu.make_async_remote_copy(
            src_ref=src, dst_ref=dst, send_sem=send_sem.at[slot], recv_sem=recv_sem.at[slot],
            device_id=peer, device_id_type=MESH,
        )

    def new_slot():
        used.append(None)
        return len(used) - 1

    sent = []

    def send(src, dst, slot, peer, when=None):
        def make():
            return copy(src(), dst(), slot, peer)

        sent.append((when, make))
        if when is None:
            make().start()
        else:
            pl.when(when)(lambda: make().start())

    def arrive(dst, slot, peer):
        copy(dst, dst, slot, peer).wait_recv()

    load = pltpu.make_async_copy(h_hbm, raw, load_sem)
    load.start()
    load.wait()

    @pl.loop(0, ROWS // ORB)
    def _(i):
        at = rows_at(i * ORB, ORB, ORB)
        for j in range(COLS // ORB):
            lanes = slice(j * ORB, (j + 1) * ORB)
            wide[at, lanes] = raw[at, lanes].astype(F32) * pat_ref[i, j].astype(F32)

    for k in range(2):
        for i in range(NX):
            stack = [wide[(s * 2 * NX + i * 2 + k) * PIECE:(s * 2 * NX + i * 2 + k + 1) * PIECE, :] for s in range(NZ)]
            at = (k * NX + i) * STACK
            ham[at:at + STACK, :] = jnp.concatenate(stack, axis=0).astype(BF16)

    def product_out(t, h, vec):
        theirs = rows_at((1 - core) * HALF, HALF, HALF)
        send_c[t, h] = jnp.dot(ham[theirs, :], vec, preferred_element_type=F32).astype(BF16)

    def product_own(h, vec):
        mine = rows_at(core * HALF, HALF, HALF)
        own[h] = jnp.dot(ham[mine, :], vec, preferred_element_type=F32)

    def to_core(t, h, slot):
        send(lambda: send_c.at[t, h], lambda: recv_c.at[t, h], slot, other)

    def along_x(t, slots_c):
        slots = {}
        for h in range(CHUNKS):
            arrive(recv_c.at[t, h], slots_c[h], other)
            for d in (2, 1, 3, 0):
                at = rows_at(plus(x, d, NX) * STACK, STACK, STACK)
                total = own[h, at, :] + recv_c[t, h, at, :].astype(F32)
                if d == 0:
                    acc[h] = total
                    continue
                send_x[t, h, d - 1] = total.astype(BF16)
                slots[h, d] = new_slot()
                send(functools.partial(lambda h, d: send_x.at[t, h, d - 1], h, d),
                     functools.partial(lambda h, d: recv_x.at[t, h, d - 1], h, d), slots[h, d], x_peer[d])
        return slots

    def add_x(t, h, slots):
        for d in (1, 3, 2):
            arrive(recv_x.at[t, h, d - 1], slots[h, d], x_peer[d])
        acc[h] = acc[h] + recv_x[t, h, 0].astype(F32) + recv_x[t, h, 1].astype(F32) + recv_x[t, h, 2].astype(F32)

    def vec_of(ref, h):
        return ref[:, h * W:(h + 1) * W]

    for h in range(CHUNKS):
        product_out(0, h, vec_of(v_ref, h))
        product_own(h, vec_of(v_ref, h))
    pl.semaphore_wait(barrier, len(everyone))
    slots_c = [new_slot() for _ in range(CHUNKS)]
    for h in range(CHUNKS):
        to_core(0, h, slots_c[h])
    slots_x = along_x(0, slots_c)

    for i in range(ROWS // ORB):
        ham_t[:, i * ORB:(i + 1) * ORB] = ham[i * ORB:(i + 1) * ORB, :].T

    def middle(at):
        return jnp.logical_and(at >= 2, at <= 5)

    base = (core * NX + x) * STACK
    slots_z = {}
    for h in range(CHUNKS):
        add_x(0, h, slots_x)
        send_z[h] = acc[h].astype(BF16)
        for d in (4, 5, 3, 6, 2, 7, 1):
            to = plus(z, d, NZ)
            slots_z[h, d] = new_slot()
            send(functools.partial(lambda h, to: send_z.at[h, rows_at((to - 2) * MIDDLE, MIDDLE, 16)], h, to),
                 functools.partial(lambda h, d: recv_z.at[h, d - 1], h, d), slots_z[h, d], z_peer[d], middle(to))

    slots_g = {}
    for h in range(CHUNKS):
        for d in range(1, NZ):
            slots_g[h, d] = new_slot()

        @pl.when(middle(z))
        def _(h=h):
            for d in range(1, NZ):
                arrive(recv_z.at[h, d - 1], slots_z[h, d], z_peer[d])
            total = acc[h, rows_at((z - 2) * MIDDLE, MIDDLE, 16), :]
            for d in range(1, NZ):
                total = total + recv_z[h, d - 1].astype(F32)
            first[h, rows_at(base + (z - 2) * MIDDLE, MIDDLE, 16), :] = total.astype(BF16)

        def own_middle(h=h):
            return first.at[h, rows_at(base + (z - 2) * MIDDLE, MIDDLE, 16)]

        for d in (4, 5, 3, 6, 2, 7, 1):
            send(own_middle, own_middle, slots_g[h, d], z_peer[d], middle(z))

    slots_gx, slots_gc = {}, {}

    def block(h, at_core, at_x):
        return first.at[h, rows_at((at_core * NX + at_x) * STACK, STACK, STACK)]

    for h in range(CHUNKS):
        for d in range(1, NZ):
            back = minus(z, d, NZ)

            @pl.when(middle(back))
            def _(h=h, d=d, back=back):
                arrive(first.at[h, rows_at(base + (back - 2) * MIDDLE, MIDDLE, 16)], slots_g[h, d], z_peer[d])

        mine = functools.partial(block, h, core, x)
        for d in (2, 1, 3):
            slots_gx[h, d] = new_slot()
            send(mine, mine, slots_gx[h, d], x_peer[d])
        slots_gc[h, 0] = new_slot()
        send(mine, mine, slots_gc[h, 0], other)
    for h in range(CHUNKS):
        for d in (1, 3, 2):
            back = minus(x, d, NX)
            theirs = functools.partial(block, h, core, back)
            arrive(theirs(), slots_gx[h, d], x_peer[d])
            slots_gc[h, d] = new_slot()
            send(theirs, theirs, slots_gc[h, d], other)

    slots_y = {}
    for h in range(CHUNKS):
        for d in range(NX):
            arrive(block(h, 1 - core, minus(x, d, NX)), slots_gc[h, d], other)
        own[h, 0:COLS, :] = jnp.dot(ham_t[...], first[h], preferred_element_type=F32)
        for d in (2, 1, 3):
            send_y[h, d - 1] = own[h, rows_at(plus(y, d, NY) * QUARTER, QUARTER, 16), :].astype(BF16)
            slots_y[h, d] = new_slot()
            send(functools.partial(lambda h, d: send_y.at[h, d - 1], h, d),
                 functools.partial(lambda h, d: recv_y.at[h, d - 1], h, d), slots_y[h, d], y_peer[d])
        accy[h] = own[h, rows_at(y * QUARTER, QUARTER, 16), :]

    def exchange_w(stage, h, slots):
        for g in range(2):
            send_w[stage, h, g] = accy[h, g * PAIR:(g + 1) * PAIR, :].astype(BF16)
            slots[stage, h, g] = new_slot()
            send(functools.partial(lambda g: send_w.at[stage, h, g], g),
                 functools.partial(lambda g: recv_w.at[stage, h, g], g), slots[stage, h, g], w_peer[(g + stage) % 2])

    def add_w(stage, h, slots):
        for g in range(2):
            arrive(recv_w.at[stage, h, g], slots[stage, h, g], w_peer[(g + stage) % 2])
            accy[h, g * PAIR:(g + 1) * PAIR, :] = accy[h, g * PAIR:(g + 1) * PAIR, :] + recv_w[stage, h, g].astype(F32)

    slots_w = {}
    for h in range(CHUNKS):
        for d in (1, 3, 2):
            arrive(recv_y.at[h, d - 1], slots_y[h, d], y_peer[d])
        accy[h] = accy[h] + recv_y[h, 0].astype(F32) + recv_y[h, 1].astype(F32) + recv_y[h, 2].astype(F32)
        exchange_w(0, h, slots_w)
    for h in range(CHUNKS):
        add_w(0, h, slots_w)
        exchange_w(1, h, slots_w)
    slots_s = {}
    quarter = rows_at(y * QUARTER, QUARTER, 16)
    for h in range(CHUNKS):
        add_w(1, h, slots_w)
        before = v_ref[quarter, h * W:(h + 1) * W].astype(F32)
        second[h, quarter, :] = (2.0 * accy[h] - before).astype(BF16)
        for d in (2, 1, 3):
            slots_s[h, d] = new_slot()
            place = functools.partial(lambda h: second.at[h, quarter], h)
            send(place, place, slots_s[h, d], y_peer[d])

    slots_c = []
    for h in range(CHUNKS):
        for d in (1, 3, 2):
            arrive(second.at[h, rows_at(minus(y, d, NY) * QUARTER, QUARTER, 16)], slots_s[h, d], y_peer[d])
        product_out(1, h, second[h])
        slots_c.append(new_slot())
        to_core(1, h, slots_c[h])
        product_own(h, second[h])
    slots_x = along_x(1, slots_c)
    for h in range(CHUNKS):
        firstw[h] = first[h, rows_at(base, STACK, STACK), :].astype(F32)

    def folded(ref, at):
        rows = rows_at(at * PIECE, PIECE, 8)
        halves = [ref[0, rows, :], ref[1, rows, :]] if CHUNKS == 2 else [ref[0, rows, :ORB], ref[0, rows, ORB:]]
        return jnp.concatenate(halves, axis=0)

    for h in range(CHUNKS):
        add_x(1, h, slots_x)
    slots_f = {}
    for d in (4, 5, 3, 6, 2, 7, 1):
        send_f[d - 1] = folded(acc, plus(z, d, NZ)).astype(BF16)
        slots_f[d] = new_slot()
        send(functools.partial(lambda d: send_f.at[d - 1], d), functools.partial(lambda d: recv_f.at[d - 1], d),
             slots_f[d], z_peer[d])
    total = folded(acc, z)
    for d in (1, 7, 2, 6, 3, 5, 4):
        arrive(recv_f.at[d - 1], slots_f[d], z_peer[d])
        total = total + recv_f[d - 1].astype(F32)
    result = 2.0 * total - folded(firstw, z)
    out_ref[:, :ORB] = result[:PIECE].astype(BF16)
    out_ref[:, ORB:] = result[PIECE:].astype(BF16)

    for when, make in sent:
        if when is None:
            make().wait_send()
        else:
            pl.when(when)(lambda make=make: make().wait_send())


def slots_needed():
    per_chunk = 2 * (1 + 3) + 2 * 7 + 3 + 4 + 3 + 4 + 3
    return CHUNKS * per_chunk + 7


def body(hamiltonian, pattern, vectors):
    vm = pltpu.VMEM
    n = CHUNKS
    scratch = [
        vm((ROWS, COLS), BF16), vm((ROWS, COLS), F32), vm((ROWS, COLS), BF16), vm((COLS, ROWS), BF16),
        vm((n, HALF, W), F32), vm((n, STACK, W), F32), vm((n, QUARTER, W), F32), vm((n, STACK, W), F32),
        vm((2, n, HALF, W), BF16), vm((2, n, HALF, W), BF16),
        vm((2, n, 3, STACK, W), BF16), vm((2, n, 3, STACK, W), BF16),
        vm((n, STACK, W), BF16), vm((n, 7, MIDDLE, W), BF16), vm((n, ROWS, W), BF16),
        vm((n, 3, QUARTER, W), BF16), vm((n, 3, QUARTER, W), BF16),
        vm((2, n, 2, PAIR, W), BF16), vm((2, n, 2, PAIR, W), BF16), vm((n, COLS, W), BF16),
        vm((7, 2 * PIECE, ORB), BF16), vm((7, 2 * PIECE, ORB), BF16),
        pltpu.SemaphoreType.DMA((slots_needed(),)), pltpu.SemaphoreType.DMA((slots_needed(),)),
        pltpu.SemaphoreType.DMA,
    ]
    return pl.pallas_call(
        kernel,
        out_shape=jax.ShapeDtypeStruct((PIECE, WIDTH), BF16),
        in_specs=[
            pl.BlockSpec(memory_space=pl.ANY),
            pl.BlockSpec(memory_space=pltpu.SMEM),
            pl.BlockSpec(memory_space=pltpu.VMEM),
        ],
        out_specs=pl.BlockSpec(memory_space=pltpu.VMEM),
        scratch_shapes=scratch,
        compiler_params=pltpu.CompilerParams(collective_id=0, has_side_effects=True, vmem_limit_bytes=40 * 2**20),
        cost_estimate=pl.CostEstimate(flops=6 * ROWS * COLS * WIDTH, bytes_accessed=2 * ROWS * COLS, transcendentals=0),
        name="filter_kernel",
    )(hamiltonian, pattern, vectors)


def solution(mesh):
    in_specs = (P("row", "col"), P("row", "col"), P("col", None))
    out_specs = P(("row", "col"), None)
    return jax.shard_map(body, mesh=mesh, in_specs=in_specs, out_specs=out_specs, check_vma=False)
```

time: 1270 us -> 92 us (0.07)
  waiting for transfers between devices: 1070 us -> 0 us
  blocking collectives: 180 us -> 0 us
  Pallas kernels: 0 us -> 87.2 us
  between operations: 13.1 us -> 0.01 us
    reduce_scatter x3 -> x0, waiting for transfers between devices: 1070 us -> none  [the longest x2 905 us: col_scatter(): lax.psum_scatter(partial_value, 'col', scatter_dimension=0, tiled=True)]
    all_gather x2 -> x0, blocking collectives: 180 us -> none  [the longest x1 114 us: body(): lax.all_gather(first_piece, 'col', axis=0, tiled=True)]
    pallas_call x0 -> x1, Pallas kernels: none -> 87.2 us  [body(): pl.pallas_call(kernel, out_shape=jax.ShapeDtypeStruct((PIECE, WIDTH), BF1...]
  transfers between devices with their start and end apart: 3 -> 0, of which waited for: 3 -> 0; matrix products, arithmetic and copies ran while one was open for 0% -> 0% of each run, Pallas kernels for 0% -> 0%
where the time goes in v1:
time: 92 us; the launch traced here: 90.8 us
  Pallas kernels  87.2 us (95%)
  local copies, waits for them, and re-layouts  3.57 us (4%)
    pallas_call x1, Pallas kernels, body(): pl.pallas_call(kernel, out_shape=jax.ShapeDtypeStruct((PIECE, WIDTH), BF1...  87.2 us
    unnamed x6, local copies, waits for them, and re-layouts  3.57 us

profile of v1, /device:TPU:24, one launch (start us, length us, event | category | flops | bytes accessed | tf_op | source)
XLA Modules:
  0.0 90.8 jit_solution(5000631884041019084)
XLA Ops:
  0.0 0.8 copy.4.pat_ref
  0.8 0.0 copy-start
  0.8 1.3 %copy-done = bf16[1536,384]{1,0:T(8,128)(2,1)S(1)} copy-done((bf16[1536,384]{1,0:T(8,128)(2,1)S(1)}, bf16[1536,384]{1,0:T(8,128)(2,1)}, u32[]{:S(2)}) %copy-start) | copy-done | bytes 1179672
  2.0 0.0 copy-start.1
  2.0 0.9 %copy-done.1 = bf16[384,256]{1,0:T(8,128)(2,1)S(1)} copy-done((bf16[384,256]{1,0:T(8,128)(2,1)S(1)}, bf16[384,256]{1,0:T(8,128)(2,1)}, u32[]{:S(2)}) %copy-start.1) | copy-done | bytes 196632
  3.0 87.2 %filter_kernel.1 = bf16[24,256]{1,0:T(8,128)(2,1)S(1)} custom-call(bf16[1536,384]{1,0:T(8,128)(2,1)S(1)} %copy-done, s32[12,3]{1,0:T(8,128)S(1)} %copy.4.pat_ref, bf16[384,256]{1,0:T(8,128)(2,1)S(1)} %copy-done.1), custom_call_target="tpu_custom_call" | custom-call | flops 905969664 | bytes 1179648 | tf_op jit(solution)/shard_map/filter_kernel/pallas_call | solution.py:317
  90.2 0.6 copy.6
Async XLA Ops:
  0.8 1.3 %copy-start = (bf16[1536,384]{1,0:T(8,128)(2,1)S(1)}, bf16[1536,384]{1,0:T(8,128)(2,1)}, u32[]{:S(2)}) copy-start(bf16[1536,384]{1,0:T(8,128)(2,1)} %h_hbm.1) | copy-start | bytes 3538948
  2.0 0.9 %copy-start.1 = (bf16[384,256]{1,0:T(8,128)(2,1)S(1)}, bf16[384,256]{1,0:T(8,128)(2,1)}, u32[]{:S(2)}) copy-start(bf16[384,256]{1,0:T(8,128)(2,1)} %v_ref.1) | copy-start | bytes 589828

commit v2 on v0

v2 whole, which is shorter than its diff:
```python
import jax
import jax.numpy as jnp
from jax import lax
from jax.experimental import pallas as pl
from jax.experimental.pallas import tpu as pltpu
from jax.sharding import PartitionSpec as P

MESH = pl.DeviceIdType.MESH
F32, BF16 = jnp.float32, jnp.bfloat16
ORB = 128
NX, NZ, NY, NW = 4, 8, 4, 4
NQ = 4
BLOCK = 384
PIECE = 24
PART = 2 * PIECE
CHUNK = NX * PART
HALF = NQ * CHUNK
ROWS = 2 * HALF
COLS = 384
WIDTH = 256
QUARTER = COLS // NY
PAIR = QUARTER // 2

C_AT = 0
X_AT = C_AT + 2 * NQ
Z_AT = X_AT + 2 * NQ * 3
G_AT = Z_AT + 7
GX_AT = G_AT + 7
GC_AT = GX_AT + NQ * 3
Y_AT = GC_AT + NQ
W_AT = Y_AT + 6
S_AT = W_AT + 8
F_AT = S_AT + 6
SLOTS = F_AT + 8


def kernel(
    h_hbm, pat_hbm, v_hbm, out_ref,
    raw, pat_ref, v_ref, wide, ham, ham_t, flat, own, acc, prod, accy, firstw, lastw,
    send_c, recv_c, send_x, recv_x, send_z, recv_z, first,
    send_y, recv_y, send_w, recv_w, second, send_f, recv_f,
    send_sem, recv_sem, load_sem,
):
    col, row = lax.axis_index("col"), lax.axis_index("row")
    core, x, z = lax.rem(col, 2), lax.rem(lax.div(col, 2), NX), lax.div(col, 2 * NX)
    y, w = lax.rem(row, NY), lax.div(row, NY)

    def device(core=core, x=x, z=z, y=y, w=w):
        return {"row": w * NY + y, "col": (z * NX + x) * 2 + core}

    def plus(at, d, n):
        return lax.rem(at + d, n)

    def minus(at, d, n):
        return lax.rem(at + n - d, n)

    def rows_at(start, size, unit):
        return pl.ds(pl.multiple_of(start, unit), size)

    other = device(core=1 - core)
    x_peer = {d: device(x=plus(x, d, NX)) for d in range(1, NX)}
    z_peer = {d: device(z=plus(z, d, NZ)) for d in range(1, NZ)}
    y_peer = {d: device(y=plus(y, d, NY)) for d in range(1, NY)}
    w_peer = [device(w=w + 1 - 2 * lax.rem(w, 2)), device(w=NW - 1 - w)]

    greeted = [other, *x_peer.values(), *y_peer.values(), *z_peer.values(), *w_peer]
    barrier = pltpu.get_barrier_semaphore()
    for peer in greeted:
        pl.semaphore_signal(barrier, inc=1, device_id=peer, device_id_type=MESH)

    sent = []

    def send(src, dst, slot, peer, when=None, recv_slot=None):
        def make():
            return pltpu.make_async_remote_copy(
                src_ref=src(), dst_ref=dst(), send_sem=send_sem.at[slot],
                recv_sem=recv_sem.at[slot if recv_slot is None else recv_slot], device_id=peer, device_id_type=MESH,
            )

        sent.append((when, make))
        if when is None:
            make().start()
        else:
            pl.when(when)(lambda: make().start())

    def all_left():
        for when, make in sent:
            if when is None:
                make().wait_send()
            else:
                pl.when(when)(lambda make=make: make().wait_send())
        sent.clear()

    def arrive(dst, slot, peer):
        pltpu.make_async_remote_copy(
            src_ref=dst, dst_ref=dst, send_sem=send_sem.at[0], recv_sem=recv_sem.at[slot],
            device_id=peer, device_id_type=MESH,
        ).wait_recv()

    low = 1 - lax.div(z, NZ // 2)

    def place_of(q):
        return low * (NQ - 1 - q) + (1 - low) * q

    far_q = [place_of(k) for k in range(NQ)]

    def chunk_rows(at_core, q):
        return rows_at((at_core * NQ + q) * CHUNK, CHUNK, CHUNK)

    def part_rows(q, at_x):
        return rows_at(((core * NQ + q) * NX + at_x) * PART, PART, PART)

    def load(k):
        at = rows_at(place_of(k) * BLOCK, BLOCK, BLOCK)
        return pltpu.make_async_copy(h_hbm.at[at], raw.at[at], load_sem.at[k])

    pat_load = pltpu.make_async_copy(pat_hbm, pat_ref, load_sem.at[NQ])
    v_load = pltpu.make_async_copy(v_hbm, v_ref, load_sem.at[NQ + 1])
    pat_load.start()
    v_load.start()
    for k in range(NQ):
        load(k).start()

    def mask(k):
        for i in range(BLOCK // ORB):
            tile = place_of(k) * (BLOCK // ORB) + i
            at = rows_at(tile * ORB, ORB, ORB)
            for j in range(COLS // ORB):
                lanes = slice(j * ORB, (j + 1) * ORB)
                raw[at, lanes] = (raw[at, lanes].astype(F32) * pat_ref[j, tile].astype(F32)).astype(BF16)

    def reorder():
        @pl.loop(0, ROWS // ORB)
        def _(i):
            at = rows_at(i * ORB, ORB, ORB)
            wide[at, :] = raw[at, :].astype(F32)

        @pl.loop(0, 2 * NQ)
        def _(n):
            k, q = lax.div(n, NQ), lax.rem(n, NQ)
            stack = []
            for i in range(NX):
                for j in range(2):
                    at = ((2 * q + j) * 2 * NX + i * 2 + k) * PIECE
                    stack.append(wide[rows_at(at, PIECE, 8), :])
            ham[rows_at(n * CHUNK, CHUNK, CHUNK), :] = jnp.concatenate(stack, axis=0).astype(BF16)

    def transpose():
        @pl.loop(0, ROWS // ORB)
        def _(n):
            k, i = lax.div(n, HALF // ORB), lax.rem(n, HALF // ORB)
            ham_t[k, :, rows_at(i * ORB, ORB, ORB)] = ham[rows_at(n * ORB, ORB, ORB), :].T

    def share(k, at_core):
        stack = []
        for i in range(NX):
            for j in range(2):
                stack.append(flat[k, rows_at((j * 2 * NX + i * 2 + at_core) * PIECE, PIECE, 8), :])
        return jnp.concatenate(stack, axis=0)

    def product_out(t, k, vec):
        send_c[t, k] = jnp.dot(ham[chunk_rows(1 - core, far_q[k]), :], vec, preferred_element_type=F32).astype(BF16)

    def product_own(k, vec):
        own[k] = jnp.dot(ham[chunk_rows(core, far_q[k]), :], vec, preferred_element_type=F32)

    def to_core(t, k):
        send(lambda: send_c.at[t, k], lambda: recv_c.at[t, k], C_AT + t * NQ + k, other)

    def along_x(t, k):
        arrive(recv_c.at[t, k], C_AT + t * NQ + k, other)
        for d in (2, 1, 3, 0):
            at = rows_at(plus(x, d, NX) * PART, PART, PART)
            total = own[k, at, :] + recv_c[t, k, at, :].astype(F32)
            if d == 0:
                acc[k] = total
                continue
            send_x[t, k, d - 1] = total.astype(BF16)
            send(lambda d=d: send_x.at[t, k, d - 1], lambda d=d: recv_x.at[t, k, d - 1],
                 X_AT + (t * NQ + k) * 3 + d - 1, x_peer[d])

    def add_x(t, k):
        for d in (1, 3, 2):
            arrive(recv_x.at[t, k, d - 1], X_AT + (t * NQ + k) * 3 + d - 1, x_peer[d])
        total = acc[k]
        for d in range(3):
            total = total + recv_x[t, k, d].astype(F32)
        acc[k] = total

    pat_load.wait()
    v_load.wait()
    vec = v_ref[...]

    @pl.loop(0, NQ)
    def _(k):
        load(k).wait()
        mask(k)
        flat[k] = jnp.dot(raw[rows_at(place_of(k) * BLOCK, BLOCK, BLOCK), :], vec, preferred_element_type=F32)
        send_c[0, k] = share(k, 1 - core).astype(BF16)

    pl.semaphore_wait(barrier, len(greeted))
    for k in range(NQ):
        to_core(0, k)

    @pl.loop(0, NQ)
    def _(k):
        own[k] = share(k, core)

    for k in range(NQ):
        along_x(0, k)
    reorder()

    def apart(to):
        return lax.rem(to - z + NZ, NZ) - 1

    in_middle = jnp.logical_and(z >= 2, z <= 5)
    for k in range(NQ):
        add_x(0, k)
        send_z[k] = acc[k].astype(BF16)
        to = far_q[k] + 2
        send(lambda k=k: send_z.at[k], lambda to=to: recv_z.at[apart(to)], Z_AT + k, device(z=to), to != z,
             Z_AT + apart(to))

    transpose()

    @pl.when(in_middle)
    def _():
        total = acc[place_of(z - 2)]
        for d in (1, 7, 2, 6, 3, 5, 4):
            arrive(recv_z.at[d - 1], Z_AT + d - 1, z_peer[d])
            total = total + recv_z[d - 1].astype(F32)
        first[part_rows(z - 2, x), :] = total.astype(BF16)

    for d in (4, 5, 3, 6, 2, 7, 1):
        send(lambda: first.at[part_rows(z - 2, x)], lambda: first.at[part_rows(z - 2, x)], G_AT + d - 1, z_peer[d],
             in_middle)

    for k in range(NQ):
        q = far_q[NQ - 1 - k]
        source = q + 2
        mine = part_rows(q, x)

        @pl.when(source != z)
        def _(source=source, mine=mine):
            arrive(first.at[mine], G_AT + lax.rem(z - source + NZ, NZ) - 1, device(z=source))

        for d in (2, 1, 3):
            send(lambda mine=mine: first.at[mine], lambda mine=mine: first.at[mine], GX_AT + k * 3 + d - 1, x_peer[d])
    for k in range(NQ):
        q = far_q[NQ - 1 - k]
        for d in (1, 3, 2):
            arrive(first.at[part_rows(q, minus(x, d, NX))], GX_AT + k * 3 + d - 1, x_peer[d])
        send(lambda q=q: first.at[chunk_rows(core, q)], lambda q=q: first.at[chunk_rows(core, q)], GC_AT + k, other)

    def half_rows(at_core):
        return rows_at(at_core * HALF, HALF, HALF)

    prod[...] = jnp.dot(ham_t[core], first[half_rows(core), :], preferred_element_type=F32)
    for k in range(NQ):
        arrive(first.at[chunk_rows(1 - core, far_q[NQ - 1 - k])], GC_AT + k, other)
    prod[...] += jnp.dot(ham_t[1 - core], first[half_rows(1 - core), :], preferred_element_type=F32)
    for h in range(2):
        lanes = slice(h * ORB, (h + 1) * ORB)
        for d in (2, 1, 3):
            send_y[h, d - 1] = prod[rows_at(plus(y, d, NY) * QUARTER, QUARTER, 16), lanes].astype(BF16)
            send(lambda h=h, d=d: send_y.at[h, d - 1], lambda h=h, d=d: recv_y.at[h, d - 1], Y_AT + h * 3 + d - 1,
                 y_peer[d])

    def w_slot(stage, h, g):
        return W_AT + (stage * 2 + h) * 2 + g

    def exchange_w(stage, h, g):
        send_w[stage, h, g] = accy[h, g * PAIR:(g + 1) * PAIR, :].astype(BF16)
        send(lambda: send_w.at[stage, h, g], lambda: recv_w.at[stage, h, g], w_slot(stage, h, g),
             w_peer[(g + stage) % 2])

    def add_w(stage, h, g):
        arrive(recv_w.at[stage, h, g], w_slot(stage, h, g), w_peer[(g + stage) % 2])
        accy[h, g * PAIR:(g + 1) * PAIR, :] += recv_w[stage, h, g].astype(F32)

    quarter = rows_at(y * QUARTER, QUARTER, 16)
    for h in range(2):
        for d in (1, 3, 2):
            arrive(recv_y.at[h, d - 1], Y_AT + h * 3 + d - 1, y_peer[d])
        total = prod[quarter, h * ORB:(h + 1) * ORB]
        for d in range(3):
            total = total + recv_y[h, d].astype(F32)
        accy[h] = total
        exchange_w(0, h, 0)
        exchange_w(0, h, 1)
    all_left()
    for h in range(2):
        for g in range(2):
            add_w(0, h, g)
            exchange_w(1, h, g)
    for h in range(2):
        lanes = slice(h * ORB, (h + 1) * ORB)
        add_w(1, h, 0)
        add_w(1, h, 1)
        second[quarter, lanes] = (2.0 * accy[h] - v_ref[quarter, lanes].astype(F32)).astype(BF16)
        for d in (2, 1, 3):
            send(lambda h=h: second.at[quarter, pl.ds(h * ORB, ORB)],
                 lambda h=h: second.at[quarter, pl.ds(h * ORB, ORB)], S_AT + h * 3 + d - 1, y_peer[d])

    for h in range(2):
        for d in (1, 3, 2):
            arrive(second.at[rows_at(minus(y, d, NY) * QUARTER, QUARTER, 16), pl.ds(h * ORB, ORB)],
                   S_AT + h * 3 + d - 1, y_peer[d])
    vec = second[...]
    for k in range(NQ):
        product_out(1, k, vec)
        to_core(1, k)
    for k in range(NQ):
        product_own(k, vec)
        along_x(1, k)
    firstw[...] = first[part_rows(lax.div(z, 2), x), :].astype(F32)

    def folded(value):
        return jnp.concatenate([value[:, :ORB], value[:, ORB:]], axis=0)

    for k in range(NQ):
        add_x(1, k)
        for j in range(2):
            n = k * 2 + j
            to = far_q[k] * 2 + j
            send_f[n] = folded(acc[k, j * PIECE:(j + 1) * PIECE, :]).astype(BF16)
            send(lambda n=n: send_f.at[n], lambda to=to: recv_f.at[apart(to)], F_AT + n, device(z=to), to != z,
                 F_AT + apart(to))
    all_left()
    odd = rows_at(lax.rem(z, 2) * PIECE, PIECE, 8)
    lastw[...] = acc[place_of(lax.div(z, 2))]
    total = folded(lastw[odd, :])
    before = folded(firstw[odd, :])
    for d in (1, 7, 2, 6, 3, 5, 4):
        arrive(recv_f.at[d - 1], F_AT + d - 1, z_peer[d])
        total = total + recv_f[d - 1].astype(F32)
    result = 2.0 * total - before
    out_ref[:, :ORB] = result[:PIECE].astype(BF16)
    out_ref[:, ORB:] = result[PIECE:].astype(BF16)


def body(hamiltonian, pattern, vectors):
    vm = pltpu.VMEM
    scratch = [
        vm((ROWS, COLS), BF16), pltpu.SMEM((COLS // ORB, ROWS // ORB), jnp.int32), vm((COLS, WIDTH), BF16),
        vm((ROWS, COLS), F32), vm((ROWS, COLS), BF16), vm((2, COLS, HALF), BF16),
        vm((NQ, BLOCK, WIDTH), F32), vm((NQ, CHUNK, WIDTH), F32), vm((NQ, PART, WIDTH), F32), vm((COLS, WIDTH), F32), vm((2, QUARTER, ORB), F32),
        vm((PART, WIDTH), F32), vm((PART, WIDTH), F32),
        vm((2, NQ, CHUNK, WIDTH), BF16), vm((2, NQ, CHUNK, WIDTH), BF16),
        vm((2, NQ, 3, PART, WIDTH), BF16), vm((2, NQ, 3, PART, WIDTH), BF16),
        vm((NQ, PART, WIDTH), BF16), vm((7, PART, WIDTH), BF16), vm((ROWS, WIDTH), BF16),
        vm((2, 3, QUARTER, ORB), BF16), vm((2, 3, QUARTER, ORB), BF16),
        vm((2, 2, 2, PAIR, ORB), BF16), vm((2, 2, 2, PAIR, ORB), BF16), vm((COLS, WIDTH), BF16),
        vm((8, PART, ORB), BF16), vm((7, PART, ORB), BF16),
        pltpu.SemaphoreType.DMA((SLOTS,)), pltpu.SemaphoreType.DMA((SLOTS,)), pltpu.SemaphoreType.DMA((NQ + 2,)),
    ]
    return pl.pallas_call(
        kernel,
        out_shape=jax.ShapeDtypeStruct((PIECE, WIDTH), BF16),
        in_specs=[pl.BlockSpec(memory_space=pl.ANY)] * 3,
        out_specs=pl.BlockSpec(memory_space=pltpu.VMEM),
        scratch_shapes=scratch,
        compiler_params=pltpu.CompilerParams(collective_id=0, has_side_effects=True, vmem_limit_bytes=60 * 2**20),
        cost_estimate=pl.CostEstimate(flops=6 * ROWS * COLS * WIDTH, bytes_accessed=2 * ROWS * COLS, transcendentals=0),
        name="filter_kernel",
    )(hamiltonian, pattern.T, vectors)


def solution(mesh):
    in_specs = (P("row", "col"), P("row", "col"), P("col", None))
    out_specs = P(("row", "col"), None)
    return jax.shard_map(body, mesh=mesh, in_specs=in_specs, out_specs=out_specs, check_vma=False)
```

time: 1270 us -> 89.4 us (0.07)
  waiting for transfers between devices: 1070 us -> 0 us
  blocking collectives: 180 us -> 0 us
  Pallas kernels: 0 us -> 87.4 us
  between operations: 13.1 us -> 0.01 us
    reduce_scatter x3 -> x0, waiting for transfers between devices: 1070 us -> none  [the longest x2 905 us: col_scatter(): lax.psum_scatter(partial_value, 'col', scatter_dimension=0, tiled=True)]
    all_gather x2 -> x0, blocking collectives: 180 us -> none  [the longest x1 114 us: body(): lax.all_gather(first_piece, 'col', axis=0, tiled=True)]
    pallas_call x0 -> x1, Pallas kernels: none -> 87.4 us  [body(): pl.pallas_call(kernel, out_shape=jax.ShapeDtypeStruct((PIECE, WIDTH), BF1...]
  transfers between devices with their start and end apart: 3 -> 0, of which waited for: 3 -> 0; matrix products, arithmetic and copies ran while one was open for 0% -> 0% of each run, Pallas kernels for 0% -> 0%
where the time goes in v2:
time: 89.4 us; the launch traced here: 88.7 us
  Pallas kernels  87.4 us (98%)
  local copies, waits for them, and re-layouts  1.31 us (1%)
    pallas_call x1, Pallas kernels, body(): pl.pallas_call(kernel, out_shape=jax.ShapeDtypeStruct((PIECE, WIDTH), BF1...  87.4 us

profile of v2, /device:TPU:24, one launch (start us, length us, event | category | flops | bytes accessed | tf_op | source)
XLA Modules:
  0.0 88.7 jit_solution(535442463095970062)
XLA Ops:
  0.0 87.4 %filter_kernel.1 = bf16[24,256]{1,0:T(8,128)(2,1)} custom-call(bf16[1536,384]{1,0:T(8,128)(2,1)} %h_hbm.1, s32[3,12]{1,0:T(4,128)} %bitcast.1, bf16[384,256]{1,0:T(8,128)(2,1)} %v_hbm.1), custom_call_target="tpu_custom_call" | custom-call | flops 905969664 | bytes 1179648 | tf_op jit(solution)/shard_map/filter_kernel/pallas_call | solution.py:357
  87.4 1.3 %copy.5 = bf16[24,256]{1,0:T(8,128)(2,1)} copy(bf16[24,256]{1,0:T(8,128)(2,1)} %filter_kernel.1) | data formatting | bytes 24576
